TPU v7x, 32 devices: a whole 2x2x4 slice. The times are simulated.
32 devices in a mesh: gx: 8 (over z, y), gy: 4 (over x, core).
Axes of the slice: x: 2, y: 2, z: 4, core: 2. Of those that a mesh axis runs over, the one named last changes fastest.
Arguments:
- atm_state: float32 [2, 72, 512, 512], P(None, None, 'gx', 'gy'), may hold values from -6 to 6
- ocean_state: float32 [2, 60, 512, 512], P(None, None, 'gx', 'gy'), may hold values from -6 to 6
- land_mask: int32 [512, 512], P('gx', 'gy'), may hold values 0 or 1
- elem_op: float32 [16, 16], replicated, may hold values from -1.5 to 1.5
- column_mix: float32 [72, 72], replicated, may hold values from -0.75 to 0.75
- kappa: float32 [2, 60], replicated, may hold values from 0.03 to 0.2
- remap_weight: bfloat16 [512, 4, 4, 128, 128], P('gx', 'gy'), may hold values from -0.5 to 0.5
- intersection: int32 [512, 4, 4], replicated, may hold values from 0 to 2047, as said below
Outputs:
- atm_next: float32 [2, 72, 512, 512], P(None, None, 'gx', 'gy')
- ocean_next: float32 [2, 60, 512, 512], P(None, None, 'gx', 'gy')
- surface_on_atm: float32 [2, 512, 512], P(None, 'gx', 'gy')
Inputs may be any that keep to these rules, and one draw needn't show every extreme that they name: `intersection`: among the 256 entries of the atmosphere points of one device (rows of one tile along the first dimension, one column block), at most 20 name blocks of any one ocean tile d = o // 64; in every draw some tile receives exactly 20 from every device.
All inputs are finite; a program needn't handle non-finite values. No bound on the sum of `land_mask` on one device may be relied on, other than what follows from the above.
Results may differ from a plain program's by a relative error of at most 0.0032.
Values may be sent and summed in bfloat16 or wider, within the bound.
A program may use at most 192 MiB of HBM per device.

v0:
```python
import jax
import jax.numpy as jnp
from jax import lax
from jax.experimental import pallas as pl
from jax.experimental.pallas import tpu as pltpu
from jax.sharding import PartitionSpec as P

OSUB = 2


ELEM_STEP = 0.5
MIX_STEP = 0.5
FLUX_GAIN = 0.25


def row_halo(planes):
    count = lax.axis_size("gx")
    before = lax.ppermute(planes[:, -1], "gx", [(i, (i + 1) % count) for i in range(count)])
    after = lax.ppermute(planes[:, 0], "gx", [((i + 1) % count, i) for i in range(count)])
    return before, after


def col_halo(first, last):
    count = lax.axis_size("gy")
    before = lax.ppermute(last, "gy", [(i, (i + 1) % count) for i in range(count)])
    after = lax.ppermute(first, "gy", [((i + 1) % count, i) for i in range(count)])
    return before, after


def neighbours(x, before, after, axis):
    count = x.shape[axis]
    place = lax.broadcasted_iota(jnp.int32, x.shape, axis)
    down = jnp.where(place == 0, before, pltpu.roll(x, 1, axis))
    up = jnp.where(place == count - 1, after, pltpu.roll(x, count - 1, axis))
    return down, up, place


def averaged(x, before, after, axis):
    down, up, place = neighbours(x, before, after, axis)
    side = place % 4
    return jnp.where(side == 3, (x + up) * 0.5, jnp.where(side == 0, (x + down) * 0.5, x))


def spread_cols(cols_ref, p, x):
    rows, cols = x.shape
    top = lax.broadcasted_iota(jnp.int32, (cols, rows), 0) == 0
    return jnp.where(top, cols_ref[p, 0:1], cols_ref[p, 1:2]).T


def put_edges(edges_ref, p, x):
    turned = x.T
    edges_ref[p, 0:1] = turned[0:1]
    edges_ref[p, 1:2] = turned[x.shape[1] - 1 :]


def edges_kernel(x_ref, edges_ref):
    for p in range(x_ref.shape[0]):
        put_edges(edges_ref, p, x_ref[p])


def stiffness_kernel(x_ref, west_ref, east_ref, cols_ref, out_ref):
    for p in range(x_ref.shape[0]):
        x = averaged(x_ref[p], west_ref[p], east_ref[p], 0)
        sides = spread_cols(cols_ref, p, x)
        out_ref[p] = averaged(x, sides, sides, 1)


def tracer_kernel(x_ref, west_ref, east_ref, cols_ref, masks_ref, kappa_ref, out_ref, *edges):
    for p in range(x_ref.shape[0]):
        x = x_ref[p]
        sides = spread_cols(cols_ref, p, x)
        western, eastern, _ = neighbours(x, west_ref[p], east_ref[p], 0)
        southern, northern, _ = neighbours(x, sides, sides, 1)
        total = masks_ref[0] * (eastern - x) + masks_ref[1] * (western - x)
        total = total + masks_ref[2] * (northern - x)
        total = total + masks_ref[3] * (southern - x)
        result = x + masks_ref[4] * (kappa_ref[p] * total)
        out_ref[p] = result
        if edges:
            put_edges(edges[0], p, result)


def plane_call(kernel, x, sides=(), extras=(), fill=True, edges=False):
    planes, rows, cols = x.shape
    step = 12 if planes % 12 == 0 else 1
    block = lambda *dims: pl.BlockSpec((step,) + dims, lambda i: (i, 0, 0))
    specs = [block(rows, cols)]
    args = [x]
    if sides:
        west, east, south, north = sides
        specs += [block(1, cols), block(1, cols), block(2, rows)]
        args += [west[:, None], east[:, None], jnp.stack([south, north], axis=1)]
    if extras:
        masks, scale = extras
        specs += [pl.BlockSpec(masks.shape, lambda i: (0, 0, 0)), block(1, cols)]
        args += [masks, scale]
    out_specs = [block(rows, cols)] * fill + [block(2, rows)] * edges
    out_shape = [jax.ShapeDtypeStruct(x.shape, x.dtype)] * fill
    out_shape += [jax.ShapeDtypeStruct((planes, 2, rows), x.dtype)] * edges
    return pl.pallas_call(
        kernel,
        grid=(planes // step,),
        in_specs=specs,
        out_specs=out_specs,
        out_shape=out_shape,
        compiler_params=pltpu.CompilerParams(vmem_limit_bytes=32 * 1024 * 1024),
    )(*args)


def split(x):
    high = x.astype(jnp.bfloat16)
    return high, (x - high.astype(jnp.float32)).astype(jnp.bfloat16)


def dot(a, b):
    return jnp.dot(a, b, preferred_element_type=jnp.float32)


def element_kernel(x_ref, op_ref, mix_ref, out_ref, held, stepped, spread_ref):
    _, levels, rows, cols = x_ref.shape
    wide = 4 * cols

    @pl.when((pl.program_id(0) == 0) & (pl.program_id(1) == 0))
    def _():
        def place(index):
            return index // cols * 4 + index % 4

        tall = place(lax.broadcasted_iota(jnp.int32, (wide, 16), 0))
        left = (tall == lax.broadcasted_iota(jnp.int32, (wide, 16), 1)).astype(jnp.float32)
        flat = place(lax.broadcasted_iota(jnp.int32, (16, wide), 1))
        right = (flat == lax.broadcasted_iota(jnp.int32, (16, wide), 0)).astype(jnp.float32)
        row = lax.broadcasted_iota(jnp.int32, (wide, wide), 0) % cols // 4
        col = lax.broadcasted_iota(jnp.int32, (wide, wide), 1) % cols // 4
        for k, piece in enumerate(split(op_ref[...])):
            half = dot(left, piece.astype(jnp.float32))
            full = dot(half, right)
            spread_ref[k] = jnp.where(row == col, full, 0.0).astype(jnp.bfloat16)

    held[...] = x_ref[0].reshape(levels * rows, cols)
    quarter = levels * rows // 4
    parts = [held[pl.ds(i, quarter, stride=4), :] for i in range(4)]
    high, low = split(jnp.concatenate(parts, axis=1))
    applied = dot(high, spread_ref[0]) + (dot(low, spread_ref[0]) + dot(high, spread_ref[1]))
    for i in range(4):
        stepped[pl.ds(i, quarter, stride=4), :] = (
            parts[i] + ELEM_STEP * applied[:, i * cols : (i + 1) * cols]
        )
    lines = [stepped[pl.ds(r, levels, stride=rows), :] for r in range(rows)]
    high, low = split(jnp.concatenate(lines, axis=1))
    mix_high, mix_low = split(mix_ref[...])
    mixed = dot(mix_high, high) + (dot(mix_low, high) + dot(mix_high, low))
    for r in range(rows):
        held[pl.ds(r, levels, stride=rows), :] = (
            lines[r] + MIX_STEP * mixed[:, r * cols : (r + 1) * cols]
        )
    out_ref[0] = held[...].reshape(levels, rows, cols)


def element_step(fields, elem_op, column_mix):
    variables, levels, row_count, col_count = fields.shape
    rows = 8
    block = pl.BlockSpec((1, levels, rows, col_count), lambda v, r: (v, 0, r, 0))
    return pl.pallas_call(
        element_kernel,
        grid=(variables, row_count // rows),
        in_specs=[
            block,
            pl.BlockSpec(elem_op.shape, lambda v, r: (0, 0)),
            pl.BlockSpec(column_mix.shape, lambda v, r: (0, 0)),
        ],
        out_specs=block,
        out_shape=jax.ShapeDtypeStruct(fields.shape, fields.dtype),
        scratch_shapes=[pltpu.VMEM((levels * rows, col_count), jnp.float32)] * 2
        + [pltpu.VMEM((2, 4 * col_count, 4 * col_count), jnp.bfloat16)],
        compiler_params=pltpu.CompilerParams(vmem_limit_bytes=32 * 1024 * 1024),
    )(fields, elem_op.T, column_mix)


def column_average(column, before, after):
    padded = jnp.concatenate([before[:, None], column, after[:, None]], axis=1)
    side = jnp.arange(column.shape[1])[None, :] % 4
    return jnp.where(
        side == 3,
        (column + padded[:, 2:]) * 0.5,
        jnp.where(side == 0, (column + padded[:, :-2]) * 0.5, column),
    )


def stiffness_sum(stepped):
    x = stepped.reshape((-1,) + stepped.shape[2:])
    west, east = row_halo(x)
    (edges,) = plane_call(edges_kernel, x, fill=False, edges=True)
    first = column_average(edges[:, 0], west[:, 0], east[:, 0])
    last = column_average(edges[:, 1], west[:, -1], east[:, -1])
    south, north = col_halo(first, last)
    (out,) = plane_call(stiffness_kernel, x, (west, east, south, north))
    return out.reshape(stepped.shape)


def ocean_halo(x, first, last, gy_index, gy_count):
    count = lax.axis_size("gx")
    west, east = row_halo(x)
    south, north = col_halo(first, last)
    mirrored = lax.ppermute(last, "gx", [(i, count - 1 - i) for i in range(count)])
    north = jnp.where(gy_index == gy_count - 1, jnp.flip(mirrored, axis=1), north)
    return west, east, south, north


def mask_set(wet, gy_index, gy_count):
    west, east, south, north = (side[0] for side in ocean_halo(wet[None], wet[None, :, 0], wet[None, :, -1], gy_index, gy_count))
    south = jnp.where(gy_index == 0, jnp.zeros_like(south), south)
    return jnp.stack(
        [
            jnp.concatenate([wet[1:], east[None]], axis=0),
            jnp.concatenate([west[None], wet[:-1]], axis=0),
            jnp.concatenate([wet[:, 1:], north[:, None]], axis=1),
            jnp.concatenate([south[:, None], wet[:, :-1]], axis=1),
            wet,
        ]
    )


def tracer_steps(tracers, masks, kappa, gy_index, gy_count):
    x = tracers.reshape((-1,) + tracers.shape[2:])
    scale = jnp.broadcast_to(kappa.reshape(-1, 1, 1), (x.shape[0], 1, x.shape[2]))
    (edges,) = plane_call(edges_kernel, x, fill=False, edges=True)
    for repeat in range(OSUB):
        halo = ocean_halo(x, edges[:, 0], edges[:, 1], gy_index, gy_count)
        if repeat < OSUB - 1:
            x, edges = plane_call(tracer_kernel, x, halo, (masks, scale), edges=True)
        else:
            (x,) = plane_call(tracer_kernel, x, halo, (masks, scale))
    return x.reshape(tracers.shape)


def per_device(
    atm_state, ocean_state, land_mask, elem_op, column_mix, kappa, remap_weight, intersection
):
    gx_count = lax.axis_size("gx")
    gy_count = lax.axis_size("gy")
    tile_count = gx_count * gy_count
    gx_index = lax.axis_index("gx")
    gy_index = lax.axis_index("gy")
    levels = atm_state.shape[1]
    atm_rows = atm_state.shape[2]
    ocean_rows = ocean_state.shape[2]
    ocean_cols = ocean_state.shape[3]
    intersections = remap_weight.shape[2]
    entries = atm_rows * intersections
    capacity = max(2, 5 * entries // (2 * tile_count))
    slot_total = tile_count * capacity
    stepped = element_step(atm_state, elem_op, column_mix)
    atm_next = stiffness_sum(stepped)
    surface = atm_next[:, levels - 1].astype(jnp.bfloat16)
    weights = remap_weight[:, 0]
    products = lax.dot_general(
        weights, surface, (((3,), (2,)), ((0,), (1,))), preferred_element_type=jnp.float32
    )
    contrib = jnp.transpose(products, (0, 1, 3, 2)).reshape(entries, 2, ocean_cols)
    own_ids = lax.dynamic_slice(
        intersection, (gx_index * atm_rows, gy_index, jnp.int32(0)), (atm_rows, 1, intersections)
    ).reshape(entries)
    target_dev = own_ids // ocean_rows
    entry_order = jnp.arange(entries)
    earlier_same = (target_dev[None, :] == target_dev[:, None]) & (
        entry_order[None, :] < entry_order[:, None]
    )
    slot_rank = jnp.sum(earlier_same.astype(jnp.int32), axis=1)
    slot_pos = target_dev * capacity + slot_rank
    send_map = (slot_pos[:, None] == jnp.arange(slot_total)[None, :]).astype(jnp.float32)
    outgoing = jnp.einsum("es,efq->sfq", send_map, contrib, precision=lax.Precision.HIGHEST)
    all_ids = jnp.transpose(
        intersection.reshape(gx_count, atm_rows, gy_count, intersections), (0, 2, 1, 3)
    ).reshape(tile_count, entries)
    own_tile = gx_index * gy_count + gy_index
    hits = (all_ids // ocean_rows == own_tile).astype(jnp.int32)
    recv_rank = jnp.cumsum(hits, axis=1) - hits
    slot_pick = (
        hits[:, :, None] * (recv_rank[:, :, None] == jnp.arange(capacity)).astype(jnp.int32)
    ).astype(jnp.float32)
    row_pick = (all_ids[:, :, None] % ocean_rows == jnp.arange(ocean_rows)).astype(jnp.float32)
    receive_map = jnp.einsum(
        "sek,sel->lsk", slot_pick, row_pick, precision=lax.Precision.HIGHEST
    ).reshape(ocean_rows, slot_total)
    incoming = lax.all_to_all(
        outgoing.reshape(tile_count, capacity, 2, ocean_cols),
        ("gx", "gy"),
        split_axis=0,
        concat_axis=0,
        tiled=True,
    )
    forcing = jnp.einsum(
        "lc,cfq->flq",
        receive_map,
        incoming.reshape(slot_total, 2, ocean_cols),
        precision=lax.Precision.HIGHEST,
    )
    wet_mask = land_mask.astype(jnp.float32)
    masks = mask_set(wet_mask, gy_index, gy_count)
    tracers = tracer_steps(ocean_state, masks, kappa, gy_index, gy_count)
    surface_level = tracers[:, 0] + wet_mask * (FLUX_GAIN * forcing)
    ocean_next = tracers.at[:, 0].set(surface_level)
    sea_surface = ocean_next[:, 0].astype(jnp.bfloat16)
    back_out = jnp.einsum(
        "lc,flq->cfq",
        receive_map.astype(jnp.bfloat16),
        sea_surface,
        preferred_element_type=jnp.float32,
    ).astype(jnp.bfloat16)
    back_in = lax.all_to_all(
        back_out.reshape(tile_count, capacity, 2, ocean_cols),
        ("gx", "gy"),
        split_axis=0,
        concat_axis=0,
        tiled=True,
    )
    entry_values = jnp.einsum(
        "es,sfq->efq",
        send_map.astype(jnp.bfloat16),
        back_in.reshape(slot_total, 2, ocean_cols),
        preferred_element_type=jnp.float32,
    )
    entry_values = entry_values.astype(jnp.bfloat16).reshape(atm_rows, intersections, 2, ocean_cols)
    returned = lax.dot_general(
        weights, entry_values, (((1, 2), (1, 3)), ((0,), (0,))), preferred_element_type=jnp.float32
    )
    surface_on_atm = jnp.transpose(returned, (2, 0, 1))
    return (atm_next, ocean_next, surface_on_atm)


def solution(mesh):
    placed = (
        P(None, None, "gx", "gy"),
        P(None, None, "gx", "gy"),
        P("gx", "gy"),
        P(),
        P(),
        P(),
        P("gx", "gy", None, None, None),
        P(),
    )
    return jax.shard_map(
        per_device,
        mesh=mesh,
        in_specs=placed,
        out_specs=(P(None, None, "gx", "gy"), P(None, None, "gx", "gy"), P(None, "gx", "gy")),
        check_vma=False,
    )
```

profile of v0, /device:TPU:0, one launch (start us, length us, event | category | flops | bytes accessed | tf_op | source)
XLA Modules:
  0.0 152.6 jit_solution(7530685238982011270)
XLA Ops:
  0.6 2.1 %copy-done.2 = f32[2,60,64,128]{3,2,1,0:T(8,128)S(1)} copy-done((f32[2,60,64,128]{3,2,1,0:T(8,128)S(1)}, f32[2,60,64,128]{3,2,1,0:T(8,128)}, u32[]{:S(2)}) %copy-start.2) | copy-done | bytes 3932184
  2.8 2.8 %shard_map.106 = f32[120,2,64]{2,1,0:T(2,128)S(1)} custom-call(f32[120,64,128]{2,1,0:T(8,128)S(1)} %bitcast.170), custom_call_target="tpu_custom_call" | custom-call | tf_op jit(solution)/shard_map/pallas_call | solution.py:100
  5.5 0.1 fusion.67
  5.6 6.1 %collective-permute-start.7 = (f32[120,64]{1,0:T(8,128)S(1)}, f32[120,64]{1,0:T(8,128)S(1)}, u32[]{:S(2)}, u32[]{:S(2)}) collective-permute-start(f32[120,64]{1,0:T(8,128)S(1)} %bitcast.195), channel_id=1, source_target_pairs={{0,28},{4,24},{8,20},{12,16},{16,12},{20,8},{24,4},{28,0},{1,29},{... | collective-permute-start | bytes 92168 | tf_op jit(solution)/shard_map/ppermute | solution.py:204
  11.7 0.8 fusion.72
  12.5 0.2 slice_reduce_fusion.1
  12.7 0.1 collective-permute-start.11
  12.8 1.6 %collective-permute-start.13 = (f32[1,64]{1,0:T(1,128)S(1)}, f32[1,64]{1,0:T(1,128)S(1)}, u32[]{:S(2)}, u32[]{:S(2)}) collective-permute-start(f32[1,64]{1,0:T(1,128)S(1)} %bitcast.203), channel_id=1, source_target_pairs={{0,1},{1,2},{2,3},{3,0},{4,5},{5,6},{6,7},{7,4},{8,9},{9,10},{10,1... | collective-permute-start | bytes 776 | tf_op jit(solution)/shard_map/ppermute | solution.py:25
  14.4 0.2 collective-permute-start.12
  14.9 0.4 copy.210
  15.3 0.7 broadcast_in_dim_reshape.3
  16.0 0.7 reshape.308
  16.7 2.3 %copy-done.6 = f32[2,72,64,128]{3,2,1,0:T(8,128)S(1)} copy-done((f32[2,72,64,128]{3,2,1,0:T(8,128)S(1)}, f32[2,72,64,128]{3,2,1,0:T(8,128)}, u32[]{:S(2)}) %copy-start.6) | copy-done | bytes 4718616
  19.1 14.4 %shard_map.103 = f32[2,72,64,128]{3,2,1,0:T(8,128)S(1)} custom-call(f32[2,72,64,128]{3,2,1,0:T(8,128)S(1)} %copy-done.6, f32[16,16]{1,0:T(8,128)S(1)} %bitcast.179, f32[72,72]{1,0:T(8,128)S(1)} %copy-done.7), custom_call_target="tpu_custom_call" | custom-call | tf_op jit(solution)/shard_map/pallas_call | solution.py:163
  33.5 2.7 %copy.185 = f32[2,72,64,128]{3,1,0,2:T(8,128)S(1)} copy(f32[2,72,64,128]{3,2,1,0:T(8,128)S(1)} %shard_map.103) | data formatting | bytes 9437184 | tf_op jit(solution)/shard_map/pallas_call | solution.py:163
  36.3 3.3 %shard_map.104 = f32[144,2,64]{2,1,0:T(2,128)S(1)} custom-call(f32[144,64,128]{2,1,0:T(8,128)S(1)} %bitcast.168), custom_call_target="tpu_custom_call" | custom-call | tf_op jit(solution)/shard_map/pallas_call | solution.py:100
  39.6 0.1 fusion.66
  39.8 0.6 reduce-window.6
  40.4 0.2 slice_reduce_fusion
  40.7 0.1 copy.206
  40.8 0.1 reshape.305
  40.9 0.2 convert_reduce_fusion
  41.2 1.2 bitcast_convert_fusion
  42.6 1.6 %collective-permute-start = (f32[144,128]{1,0:T(8,128)S(1)}, f32[144,128]{1,0:T(8,128)S(1)}, u32[]{:S(2)}, u32[]{:S(2)}) collective-permute-start(f32[144,128]{1,0:T(8,128)S(1)} %get-tuple-element.42), channel_id=1, source_target_pairs={{0,4},{4,8},{8,12},{12,16},{16,20},{20,24},{24,28},{28,0},{1,5},{5... | collective-permute-start | bytes 221192 | tf_op jit(solution)/shard_map/ppermute | solution.py:18
  44.3 3.2 %collective-permute-start.1 = (f32[144,128]{1,0:T(8,128)S(1)}, f32[144,128]{1,0:T(8,128)S(1)}, u32[]{:S(2)}, u32[]{:S(2)}) collective-permute-start(f32[144,128]{1,0:T(8,128)S(1)} %get-tuple-element.41), channel_id=1, source_target_pairs={{4,0},{8,4},{12,8},{16,12},{20,16},{24,20},{28,24},{0,28},{5,1},{9... | collective-permute-start | bytes 221192 | tf_op jit(solution)/shard_map/ppermute | solution.py:19
  47.5 1.9 %collective-permute-start.9 = (f32[1,128]{1,0:T(1,128)S(1)}, f32[1,128]{1,0:T(1,128)S(1)}, u32[]{:S(2)}, u32[]{:S(2)}) collective-permute-start(f32[1,128]{1,0:T(1,128)S(1)} %get-tuple-element.61), channel_id=1, source_target_pairs={{4,0},{8,4},{12,8},{16,12},{20,16},{24,20},{28,24},{0,28},{5,1},{9... | collective-permute-start | bytes 1544 | tf_op jit(solution)/shard_map/ppermute | solution.py:19
  49.4 0.1 copy.197
  49.6 1.4 collective-permute-done.9
  51.0 6.2 %collective-permute-done.10 = f32[1,128]{1,0:T(1,128)S(1)} collective-permute-done((f32[1,128]{1,0:T(1,128)S(1)}, f32[1,128]{1,0:T(1,128)S(1)}, u32[]{:S(2)}, u32[]{:S(2)}) %collective-permute-start.10) | collective-permute-done | bytes 544 | tf_op jit(solution)/shard_map/ppermute | solution.py:18
  57.5 0.2 fusion.40
  57.8 0.5 collective-permute-start.2
  58.4 1.4 collective-permute-done.3
  59.8 4.7 %collective-permute-start.5 = (f32[120,128]{1,0:T(8,128)S(1)}, f32[120,128]{1,0:T(8,128)S(1)}, u32[]{:S(2)}, u32[]{:S(2)}) collective-permute-start(f32[120,128]{1,0:T(8,128)S(1)} %bitcast.199), channel_id=1, source_target_pairs={{4,0},{8,4},{12,8},{16,12},{20,16},{24,20},{28,24},{0,28},{5,1},{9... | collective-permute-start | bytes 184328 | tf_op jit(solution)/shard_map/ppermute | solution.py:19
  64.5 1.5 collective-permute-start.8
  66.0 0.2 pad_maximum_fusion.cols_ref
  66.2 2.3 %copy-done.1 = f32[2,72,64,128]{3,2,1,0:T(8,128)S(1)} copy-done((f32[2,72,64,128]{3,2,1,0:T(8,128)S(1)}, f32[2,72,64,128]{3,2,1,0:T(8,128)}, u32[]{:S(2)}) %copy-start.1) | copy-done | bytes 4718616
  68.5 7.9 %shard_map.105 = f32[144,64,128]{2,1,0:T(8,128)} custom-call(f32[144,64,128]{2,1,0:T(8,128)S(1)} %bitcast.169, f32[144,1,128]{2,1,0:T(1,128)S(1)} %bitcast.173, f32[144,1,128]{2,1,0:T(1,128)S(1)} %bitcast.174, f32[144,2,64]{2,1,0:T(2,128)S(1)} %pad_maximum_fusion.cols_ref), custom_call_target="tpu_custom_call" | custom-call | tf_op jit(solution)/shard_map/pallas_call | solution.py:100
  76.4 0.8 slice.204
  77.2 5.6 %fusion.2 = f32[64,2,4,128]{3,1,2,0:T(2,128)S(1)} fusion(bf16[64,1,4,128,128]{4,3,2,1,0:T(8,128)(2,1)} %param.16, bf16[2,1,64,128]{3,2,1,0:T(8,128)(2,1)S(1)} %slice.204), kind=kOutput, calls=%fused_computation.2 | convolution fusion | flops 16777216 | bytes 8683520 | tf_op jit(solution)/shard_map/dot_general | solution.py:256
  82.9 0.5 fusion.13
  83.4 1.3 copy.209
  84.7 2.9 %all-to-all-start = ((f32[32,20,2,128]{3,2,1,0:T(2,128)}), f32[32,20,2,128]{3,2,1,0:T(2,128)S(1)}, u32[]{:S(2)}, u32[]{:S(2)}) async-start(f32[32,20,2,128]{3,2,1,0:T(2,128)} %copy.209), calls=%async_computation | async-start | bytes 1310720 | tf_op jit(solution)/shard_map/all_to_all | solution.py:285
  87.9 0.2 broadcast_in_dim.77.kappa_ref
  88.1 2.1 %copy-done.3 = f32[2,60,64,128]{3,2,1,0:T(8,128)S(1)} copy-done((f32[2,60,64,128]{3,2,1,0:T(8,128)S(1)}, f32[2,60,64,128]{3,2,1,0:T(8,128)}, u32[]{:S(2)}) %copy-start.3) | copy-done | bytes 3932184
  90.2 9.4 %shard_map.107 = (f32[120,64,128]{2,1,0:T(8,128)S(1)}, f32[120,2,64]{2,1,0:T(2,128)S(1)}) custom-call(f32[120,64,128]{2,1,0:T(8,128)S(1)} %bitcast.172, f32[120,1,128]{2,1,0:T(1,128)S(1)} %bitcast.175, f32[120,1,128]{2,1,0:T(1,128)S(1)} %bitcast.176, f32[120,2,64]{2,1,0:T(2,128)S(1)} %copy.199.cols_ref, ...), custom_call_target="tpu_custom_call" | custom-call | tf_op jit(solution)/shard_map/pallas_call | solution.py:100
  99.6 4.6 %collective-permute-start.17 = (f32[120,64]{1,0:T(8,128)S(1)}, f32[120,64]{1,0:T(8,128)S(1)}, u32[]{:S(2)}, u32[]{:S(2)}) collective-permute-start(f32[120,64]{1,0:T(8,128)S(1)} %get-tuple-element.50), channel_id=1, source_target_pairs={{0,28},{4,24},{8,20},{12,16},{16,12},{20,8},{24,4},{28,0},{1,29},{... | collective-permute-start | bytes 92168 | tf_op jit(solution)/shard_map/ppermute | solution.py:204
  104.3 2.3 %copy.200 = f32[120,64,128]{2,0,1:T(8,128)S(1)} copy(f32[120,64,128]{2,1,0:T(8,128)S(1)} %get-tuple-element.17.x_ref) | data formatting | bytes 7864320 | tf_op jit(solution)/shard_map/pallas_call | solution.py:100
  106.6 1.9 %copy-done.4 = f32[120,64,128]{2,1,0:T(8,128)} copy-done((f32[120,64,128]{2,1,0:T(8,128)}, f32[120,64,128]{2,1,0:T(8,128)S(1)}, u32[]{:S(2)}) %copy-start.4) | copy-done | bytes 3932184
  108.5 1.7 %collective-permute-start.18 = (f32[120,64]{1,0:T(8,128)S(1)}, f32[120,64]{1,0:T(8,128)S(1)}, u32[]{:S(2)}, u32[]{:S(2)}) collective-permute-start(f32[120,64]{1,0:T(8,128)S(1)} %get-tuple-element.49), channel_id=1, source_target_pairs={{1,0},{2,1},{3,2},{0,3},{5,4},{6,5},{7,6},{4,7},{9,8},{10,9},{11,1... | collective-permute-start | bytes 92168 | tf_op jit(solution)/shard_map/ppermute | solution.py:26
  110.2 0.6 collective-permute-start.14
  110.8 4.2 %collective-permute-start.15 = (f32[120,128]{1,0:T(8,128)S(1)}, f32[120,128]{1,0:T(8,128)S(1)}, u32[]{:S(2)}, u32[]{:S(2)}) collective-permute-start(f32[120,128]{1,0:T(8,128)S(1)} %get-tuple-element.43), channel_id=1, source_target_pairs={{4,0},{8,4},{12,8},{16,12},{20,16},{24,20},{28,24},{0,28},{5,1},{9... | collective-permute-start | bytes 184328 | tf_op jit(solution)/shard_map/ppermute | solution.py:19
  115.1 0.1 pad_maximum_fusion.2.cols_ref
  115.3 1.9 %collective-permute-done.14 = f32[120,128]{1,0:T(8,128)S(1)} collective-permute-done((f32[120,128]{1,0:T(8,128)S(1)}, f32[120,128]{1,0:T(8,128)S(1)}, u32[]{:S(2)}, u32[]{:S(2)}) %collective-permute-start.14) | collective-permute-done | bytes 61472 | tf_op jit(solution)/shard_map/ppermute | solution.py:18
  117.2 2.1 %copy-done.5 = f32[120,64,128]{2,1,0:T(8,128)S(1)} copy-done((f32[120,64,128]{2,1,0:T(8,128)S(1)}, f32[120,64,128]{2,1,0:T(8,128)}, u32[]{:S(2)}) %copy-start.5) | copy-done | bytes 3932184
  119.3 6.7 %shard_map.108 = f32[120,64,128]{2,1,0:T(8,128)} custom-call(f32[120,64,128]{2,1,0:T(8,128)S(1)} %copy-done.5, f32[120,1,128]{2,1,0:T(1,128)S(1)} %bitcast.177, f32[120,1,128]{2,1,0:T(1,128)S(1)} %bitcast.178, f32[120,2,64]{2,1,0:T(2,128)S(1)} %pad_maximum_fusion.2.cols_ref, f32[5,64,128]{2,1,0:T(8,128)S(1)} %constant_dynamic-update-slice_fusion.masks_ref, ...), custom_call_target="tpu_custom_call" | custom-call | tf_op jit(solution)/shard_map/pallas_call | solution.py:100
  126.0 1.7 %fusion.43 = f32[2,64,128]{2,1,0:T(8,128)S(1)} fusion(f32[2,60,64,128]{3,2,1,0:T(8,128)} %bitcast.185, f32[64,128]{1,0:T(8,128)S(1)} %broadcast_multiply_fusion, f32[32,64,20]{1,2,0:T(8,128)S(1)} %get-tuple-element.69, f32[32,20,2,128]{3,2,1,0:T(2,128)S(1)} %all-to-all-done), kind=kOutput, calls=%fused_computation.61 | convolution fusion | flops 125861888 | bytes 983040 | tf_op jit(solution)/shard_map/lc,cfq->flq/dot_general | solution.py:292
  127.7 0.2 convolution_convert_fusion
  127.9 1.1 copy.219
  129.0 6.0 %all-to-all-start.1 = ((bf16[32,20,2,128]{3,2,1,0:T(2,128)(2,1)}), bf16[32,20,2,128]{3,2,1,0:T(2,128)(2,1)S(1)}, u32[]{:S(2)}, u32[]{:S(2)}) async-start(bf16[32,20,2,128]{3,2,1,0:T(2,128)(2,1)} %bitcast.64), calls=%async_computation.1 | async-start | bytes 655360 | tf_op jit(solution)/shard_map/all_to_all | solution.py:310
  135.0 0.6 bitcast_dynamic-update-slice_fusion
  135.6 11.4 %all-to-all-done.1 = bf16[32,20,2,128]{3,2,1,0:T(2,128)(2,1)S(1)} async-done(((bf16[32,20,2,128]{3,2,1,0:T(2,128)(2,1)}), bf16[32,20,2,128]{3,2,1,0:T(2,128)(2,1)S(1)}, u32[]{:S(2)}, u32[]{:S(2)}) %all-to-all-start.1) | async-done | bytes 327712 | tf_op jit(solution)/shard_map/all_to_all | solution.py:310
  147.0 0.3 convolution_convert_fusion.1
  147.3 4.7 %fusion.5 = f32[2,64,128]{2,0,1:T(2,128)S(1)} fusion(bf16[64,1,4,128,128]{4,3,2,1,0:T(8,128)(2,1)} %param.16, bf16[64,4,2,128]{3,1,0,2:T(4,128)(2,1)S(1)} %bitcast.188), kind=kOutput, calls=%fused_computation.8 | convolution fusion | flops 16777216 | bytes 8585216 | tf_op jit(solution)/shard_map/dot_general | solution.py:324
  152.0 0.6 copy.222
  (78 shorter events, 1.7 us)
Async XLA Ops:
  0.6 2.1 %copy-start.2 = (f32[2,60,64,128]{3,2,1,0:T(8,128)S(1)}, f32[2,60,64,128]{3,2,1,0:T(8,128)}, u32[]{:S(2)}) copy-start(f32[2,60,64,128]{3,2,1,0:T(8,128)} %param.11) | copy-start | bytes 11796484
  2.7 12.0 %copy-start.8 = (s32[64,128]{1,0:T(8,128)S(1)}, s32[64,128]{1,0:T(8,128)}, u32[]{:S(2)}) copy-start(s32[64,128]{1,0:T(8,128)} %param.12) | copy-start | bytes 98308
  2.7 12.0 %copy-start.9 = (s32[512,4,4]{0,2,1:T(4,128)S(1)}, s32[512,4,4]{0,2,1:T(4,128)}, u32[]{:S(2)}) copy-start(s32[512,4,4]{0,2,1:T(4,128)} %param.17) | copy-start | bytes 98308
  2.8 13.9 %copy-start.10 = (f32[16,16]{1,0:T(8,128)S(1)}, f32[16,16]{1,0:T(8,128)}, u32[]{:S(2)}) copy-start(f32[16,16]{1,0:T(8,128)} %param.13) | copy-start | bytes 3076
  2.8 14.0 %copy-start.7 = (f32[72,72]{1,0:T(8,128)S(1)}, f32[72,72]{1,0:T(8,128)}, u32[]{:S(2)}) copy-start(f32[72,72]{1,0:T(8,128)} %mix_ref.1) | copy-start | bytes 62212
  5.6 82.0 %collective-permute-start.7 = (f32[120,64]{1,0:T(8,128)S(1)}, f32[120,64]{1,0:T(8,128)S(1)}, u32[]{:S(2)}, u32[]{:S(2)}) collective-permute-start(f32[120,64]{1,0:T(8,128)S(1)} %bitcast.195), channel_id=1, source_target_pairs={{0,28},{4,24},{8,20},{12,16},{16,12},{20,8},{24,4},{28,0},{1,29},{... | collective-permute-start | bytes 92168 | tf_op jit(solution)/shard_map/ppermute | solution.py:204
  11.7 76.1 %collective-permute-start.6 = (f32[120,64]{1,0:T(8,128)S(1)}, f32[120,64]{1,0:T(8,128)S(1)}, u32[]{:S(2)}, u32[]{:S(2)}) collective-permute-start(f32[120,64]{1,0:T(8,128)S(1)} %bitcast.196), channel_id=1, source_target_pairs={{0,1},{1,2},{2,3},{3,0},{4,5},{5,6},{6,7},{7,4},{8,9},{9,10},{10,1... | collective-permute-start | bytes 92168 | tf_op jit(solution)/shard_map/ppermute | solution.py:25
  12.7 29.9 %collective-permute-start.11 = (f32[1,64]{1,0:T(1,128)S(1)}, f32[1,64]{1,0:T(1,128)S(1)}, u32[]{:S(2)}, u32[]{:S(2)}) collective-permute-start(f32[1,64]{1,0:T(1,128)S(1)} %bitcast.202), channel_id=1, source_target_pairs={{0,28},{4,24},{8,20},{12,16},{16,12},{20,8},{24,4},{28,0},{1,29},{... | collective-permute-start | bytes 776 | tf_op jit(solution)/shard_map/ppermute | solution.py:204
  12.8 34.7 %collective-permute-start.13 = (f32[1,64]{1,0:T(1,128)S(1)}, f32[1,64]{1,0:T(1,128)S(1)}, u32[]{:S(2)}, u32[]{:S(2)}) collective-permute-start(f32[1,64]{1,0:T(1,128)S(1)} %bitcast.203), channel_id=1, source_target_pairs={{0,1},{1,2},{2,3},{3,0},{4,5},{5,6},{6,7},{7,4},{8,9},{9,10},{10,1... | collective-permute-start | bytes 776 | tf_op jit(solution)/shard_map/ppermute | solution.py:25
  14.4 29.9 %collective-permute-start.12 = (f32[1,64]{1,0:T(1,128)S(1)}, f32[1,64]{1,0:T(1,128)S(1)}, u32[]{:S(2)}, u32[]{:S(2)}) collective-permute-start(f32[1,64]{1,0:T(1,128)S(1)} %bitcast.204), channel_id=1, source_target_pairs={{1,0},{2,1},{3,2},{0,3},{5,4},{6,5},{7,6},{4,7},{9,8},{10,9},{11,1... | collective-permute-start | bytes 776 | tf_op jit(solution)/shard_map/ppermute | solution.py:26
  16.7 2.3 %copy-start.6 = (f32[2,72,64,128]{3,2,1,0:T(8,128)S(1)}, f32[2,72,64,128]{3,2,1,0:T(8,128)}, u32[]{:S(2)}) copy-start(f32[2,72,64,128]{3,2,1,0:T(8,128)} %x_ref.1) | copy-start | bytes 14155780
  33.5 2.8 %copy-start = (f32[2,72,64,128]{3,2,1,0:T(8,128)}, f32[2,72,64,128]{3,2,1,0:T(8,128)S(1)}, u32[]{:S(2)}) copy-start(f32[2,72,64,128]{3,2,1,0:T(8,128)S(1)} %shard_map.103) | copy-start | bytes 14155780
  36.3 6.2 %copy-start.11 = (f32[2,60]{1,0:T(2,128)S(1)}, f32[2,60]{1,0:T(2,128)}, u32[]{:S(2)}) copy-start(f32[2,60]{1,0:T(2,128)} %param.15) | copy-start | bytes 1444
  42.6 14.8 %collective-permute-start = (f32[144,128]{1,0:T(8,128)S(1)}, f32[144,128]{1,0:T(8,128)S(1)}, u32[]{:S(2)}, u32[]{:S(2)}) collective-permute-start(f32[144,128]{1,0:T(8,128)S(1)} %get-tuple-element.42), channel_id=1, source_target_pairs={{0,4},{4,8},{8,12},{12,16},{16,20},{20,24},{24,28},{28,0},{1,5},{5... | collective-permute-start | bytes 221192 | tf_op jit(solution)/shard_map/ppermute | solution.py:18
  44.3 13.1 %collective-permute-start.1 = (f32[144,128]{1,0:T(8,128)S(1)}, f32[144,128]{1,0:T(8,128)S(1)}, u32[]{:S(2)}, u32[]{:S(2)}) collective-permute-start(f32[144,128]{1,0:T(8,128)S(1)} %get-tuple-element.41), channel_id=1, source_target_pairs={{4,0},{8,4},{12,8},{16,12},{20,16},{24,20},{28,24},{0,28},{5,1},{9... | collective-permute-start | bytes 221192 | tf_op jit(solution)/shard_map/ppermute | solution.py:19
  47.5 3.5 %collective-permute-start.9 = (f32[1,128]{1,0:T(1,128)S(1)}, f32[1,128]{1,0:T(1,128)S(1)}, u32[]{:S(2)}, u32[]{:S(2)}) collective-permute-start(f32[1,128]{1,0:T(1,128)S(1)} %get-tuple-element.61), channel_id=1, source_target_pairs={{4,0},{8,4},{12,8},{16,12},{20,16},{24,20},{28,24},{0,28},{5,1},{9... | collective-permute-start | bytes 1544 | tf_op jit(solution)/shard_map/ppermute | solution.py:19
  51.0 6.2 %collective-permute-start.10 = (f32[1,128]{1,0:T(1,128)S(1)}, f32[1,128]{1,0:T(1,128)S(1)}, u32[]{:S(2)}, u32[]{:S(2)}) collective-permute-start(f32[1,128]{1,0:T(1,128)S(1)} %get-tuple-element.60), channel_id=1, source_target_pairs={{0,4},{4,8},{8,12},{12,16},{16,20},{20,24},{24,28},{28,0},{1,5},{5... | collective-permute-start | bytes 1544 | tf_op jit(solution)/shard_map/ppermute | solution.py:18
  57.3 30.6 %collective-permute-start.4 = (f32[120,128]{1,0:T(8,128)S(1)}, f32[120,128]{1,0:T(8,128)S(1)}, u32[]{:S(2)}, u32[]{:S(2)}) collective-permute-start(f32[120,128]{1,0:T(8,128)S(1)} %bitcast.200), channel_id=1, source_target_pairs={{0,4},{4,8},{8,12},{12,16},{16,20},{20,24},{24,28},{28,0},{1,5},{5... | collective-permute-start | bytes 184328 | tf_op jit(solution)/shard_map/ppermute | solution.py:18
  57.7 2.0 %collective-permute-start.3 = (f32[144,64]{1,0:T(8,128)S(1)}, f32[144,64]{1,0:T(8,128)S(1)}, u32[]{:S(2)}, u32[]{:S(2)}) collective-permute-start(f32[144,64]{1,0:T(8,128)S(1)} %get-tuple-element.67), channel_id=1, source_target_pairs={{1,0},{2,1},{3,2},{0,3},{5,4},{6,5},{7,6},{4,7},{9,8},{10,9},{11,1... | collective-permute-start | bytes 110600 | tf_op jit(solution)/shard_map/ppermute | solution.py:26
  57.8 6.7 %collective-permute-start.2 = (f32[144,64]{1,0:T(8,128)S(1)}, f32[144,64]{1,0:T(8,128)S(1)}, u32[]{:S(2)}, u32[]{:S(2)}) collective-permute-start(f32[144,64]{1,0:T(8,128)S(1)} %get-tuple-element.66), channel_id=1, source_target_pairs={{0,1},{1,2},{2,3},{3,0},{4,5},{5,6},{6,7},{7,4},{8,9},{9,10},{10,1... | collective-permute-start | bytes 110600 | tf_op jit(solution)/shard_map/ppermute | solution.py:25
  59.8 28.1 %collective-permute-start.5 = (f32[120,128]{1,0:T(8,128)S(1)}, f32[120,128]{1,0:T(8,128)S(1)}, u32[]{:S(2)}, u32[]{:S(2)}) collective-permute-start(f32[120,128]{1,0:T(8,128)S(1)} %bitcast.199), channel_id=1, source_target_pairs={{4,0},{8,4},{12,8},{16,12},{20,16},{24,20},{28,24},{0,28},{5,1},{9... | collective-permute-start | bytes 184328 | tf_op jit(solution)/shard_map/ppermute | solution.py:19
  64.5 23.3 %collective-permute-start.8 = (f32[120,64]{1,0:T(8,128)S(1)}, f32[120,64]{1,0:T(8,128)S(1)}, u32[]{:S(2)}, u32[]{:S(2)}) collective-permute-start(f32[120,64]{1,0:T(8,128)S(1)} %bitcast.198), channel_id=1, source_target_pairs={{1,0},{2,1},{3,2},{0,3},{5,4},{6,5},{7,6},{4,7},{9,8},{10,9},{11,1... | collective-permute-start | bytes 92168 | tf_op jit(solution)/shard_map/ppermute | solution.py:26
  66.2 2.3 %copy-start.1 = (f32[2,72,64,128]{3,2,1,0:T(8,128)S(1)}, f32[2,72,64,128]{3,2,1,0:T(8,128)}, u32[]{:S(2)}) copy-start(f32[2,72,64,128]{3,2,1,0:T(8,128)} %copy-done) | copy-start | bytes 14155780
  84.7 41.3 %all-to-all-start = ((f32[32,20,2,128]{3,2,1,0:T(2,128)}), f32[32,20,2,128]{3,2,1,0:T(2,128)S(1)}, u32[]{:S(2)}, u32[]{:S(2)}) async-start(f32[32,20,2,128]{3,2,1,0:T(2,128)} %copy.209), calls=%async_computation | async-start | bytes 1310720 | tf_op jit(solution)/shard_map/all_to_all | solution.py:285
  88.1 2.1 %copy-start.3 = (f32[2,60,64,128]{3,2,1,0:T(8,128)S(1)}, f32[2,60,64,128]{3,2,1,0:T(8,128)}, u32[]{:S(2)}) copy-start(f32[2,60,64,128]{3,2,1,0:T(8,128)} %param.11) | copy-start | bytes 11796484
  99.6 15.4 %collective-permute-start.17 = (f32[120,64]{1,0:T(8,128)S(1)}, f32[120,64]{1,0:T(8,128)S(1)}, u32[]{:S(2)}, u32[]{:S(2)}) collective-permute-start(f32[120,64]{1,0:T(8,128)S(1)} %get-tuple-element.50), channel_id=1, source_target_pairs={{0,28},{4,24},{8,20},{12,16},{16,12},{20,8},{24,4},{28,0},{1,29},{... | collective-permute-start | bytes 92168 | tf_op jit(solution)/shard_map/ppermute | solution.py:204
  104.3 10.9 %collective-permute-start.16 = (f32[120,64]{1,0:T(8,128)S(1)}, f32[120,64]{1,0:T(8,128)S(1)}, u32[]{:S(2)}, u32[]{:S(2)}) collective-permute-start(f32[120,64]{1,0:T(8,128)S(1)} %get-tuple-element.50), channel_id=1, source_target_pairs={{0,1},{1,2},{2,3},{3,0},{4,5},{5,6},{6,7},{7,4},{8,9},{9,10},{10,1... | collective-permute-start | bytes 92168 | tf_op jit(solution)/shard_map/ppermute | solution.py:25
  106.5 1.9 %copy-start.4 = (f32[120,64,128]{2,1,0:T(8,128)}, f32[120,64,128]{2,1,0:T(8,128)S(1)}, u32[]{:S(2)}) copy-start(f32[120,64,128]{2,1,0:T(8,128)S(1)} %get-tuple-element.17.x_ref) | copy-start | bytes 11796484
  108.5 6.6 %collective-permute-start.18 = (f32[120,64]{1,0:T(8,128)S(1)}, f32[120,64]{1,0:T(8,128)S(1)}, u32[]{:S(2)}, u32[]{:S(2)}) collective-permute-start(f32[120,64]{1,0:T(8,128)S(1)} %get-tuple-element.49), channel_id=1, source_target_pairs={{1,0},{2,1},{3,2},{0,3},{5,4},{6,5},{7,6},{4,7},{9,8},{10,9},{11,1... | collective-permute-start | bytes 92168 | tf_op jit(solution)/shard_map/ppermute | solution.py:26
  110.2 7.0 %collective-permute-start.14 = (f32[120,128]{1,0:T(8,128)S(1)}, f32[120,128]{1,0:T(8,128)S(1)}, u32[]{:S(2)}, u32[]{:S(2)}) collective-permute-start(f32[120,128]{1,0:T(8,128)S(1)} %get-tuple-element.44), channel_id=1, source_target_pairs={{0,4},{4,8},{8,12},{12,16},{16,20},{20,24},{24,28},{28,0},{1,5},{5... | collective-permute-start | bytes 184328 | tf_op jit(solution)/shard_map/ppermute | solution.py:18
  110.8 6.4 %collective-permute-start.15 = (f32[120,128]{1,0:T(8,128)S(1)}, f32[120,128]{1,0:T(8,128)S(1)}, u32[]{:S(2)}, u32[]{:S(2)}) collective-permute-start(f32[120,128]{1,0:T(8,128)S(1)} %get-tuple-element.43), channel_id=1, source_target_pairs={{4,0},{8,4},{12,8},{16,12},{20,16},{24,20},{28,24},{0,28},{5,1},{9... | collective-permute-start | bytes 184328 | tf_op jit(solution)/shard_map/ppermute | solution.py:19
  117.2 2.1 %copy-start.5 = (f32[120,64,128]{2,1,0:T(8,128)S(1)}, f32[120,64,128]{2,1,0:T(8,128)}, u32[]{:S(2)}) copy-start(f32[120,64,128]{2,1,0:T(8,128)} %copy-done.4) | copy-start | bytes 11796484
  129.0 18.0 %all-to-all-start.1 = ((bf16[32,20,2,128]{3,2,1,0:T(2,128)(2,1)}), bf16[32,20,2,128]{3,2,1,0:T(2,128)(2,1)S(1)}, u32[]{:S(2)}, u32[]{:S(2)}) async-start(bf16[32,20,2,128]{3,2,1,0:T(2,128)(2,1)} %bitcast.64), calls=%async_computation.1 | async-start | bytes 655360 | tf_op jit(solution)/shard_map/all_to_all | solution.py:310
where the time goes:
time: 153 us
  Pallas kernels  44.4 us (29%)
  starting transfers between devices  41.5 us (27%)
  local copies, waits for them, and re-layouts  26.5 us (17%)
  waiting for transfers between devices  22.4 us (15%)
  matrix products  14.2 us (9%)
  other arithmetic  2.44 us (2%)
    pallas_call x5, Pallas kernels, plane_call(): pl.pallas_call(kernel, grid=(planes // step,), in_specs=specs, out_specs=...  30 us
    pallas_call x1, Pallas kernels, element_step(): pl.pallas_call(element_kernel, grid=(variables, row_count // rows), in_sp...  14.4 us
    ppermute x4, starting transfers between devices, row_halo(): lax.ppermute(planes[:, 0], 'gx', [((i + 1) % count, i) for i in range(cou...  14 us
    unnamed x26, local copies, waits for them, and re-layouts  13.7 us
    all_to_all x1, waiting for transfers between devices, per_device(): lax.all_to_all(back_out.reshape(tile_count, capacity, 2, ocean_cols), ('g...  11.4 us
    ppermute x3, starting transfers between devices, ocean_halo(): lax.ppermute(last, 'gx', [(i, count - 1 - i) for i in range(count)])  10.8 us
    ppermute x4, waiting for transfers between devices, row_halo(): lax.ppermute(planes[:, -1], 'gx', [(i, (i + 1) % count) for i in range(co...  8.16 us
    all_to_all x1, starting transfers between devices, per_device(): lax.all_to_all(back_out.reshape(tile_count, capacity, 2, ocean_cols), ('g...  6 us
  transfers between devices with their start and end apart: 21, of which 5 were waited for; matrix products, arithmetic and copies ran while one was open for 14% of the time, Pallas kernels for 27%

commit v1 on v0

--- a/solution.py
+++ b/solution.py
@@ -13,10 +13,10 @@
 FLUX_GAIN = 0.25
 
 
-def row_halo(planes):
+def row_halo(first, last):
     count = lax.axis_size("gx")
-    before = lax.ppermute(planes[:, -1], "gx", [(i, (i + 1) % count) for i in range(count)])
-    after = lax.ppermute(planes[:, 0], "gx", [((i + 1) % count, i) for i in range(count)])
+    before = lax.ppermute(last, "gx", [(i, (i + 1) % count) for i in range(count)])
+    after = lax.ppermute(first, "gx", [((i + 1) % count, i) for i in range(count)])
     return before, after
 
 
@@ -47,15 +47,17 @@
     return jnp.where(top, cols_ref[p, 0:1], cols_ref[p, 1:2]).T
 
 
-def put_edges(edges_ref, p, x):
+def put_edges(edges_ref, lines_ref, p, x):
+    lines_ref[p, 0:1] = x[0:1]
+    lines_ref[p, 1:2] = x[x.shape[0] - 1 :]
     turned = x.T
     edges_ref[p, 0:1] = turned[0:1]
     edges_ref[p, 1:2] = turned[x.shape[1] - 1 :]
 
 
-def edges_kernel(x_ref, edges_ref):
+def edges_kernel(x_ref, edges_ref, lines_ref):
     for p in range(x_ref.shape[0]):
-        put_edges(edges_ref, p, x_ref[p])
+        put_edges(edges_ref, lines_ref, p, x_ref[p])
 
 
 def stiffness_kernel(x_ref, west_ref, east_ref, cols_ref, out_ref):
@@ -77,7 +79,7 @@
         result = x + masks_ref[4] * (kappa_ref[p] * total)
         out_ref[p] = result
         if edges:
-            put_edges(edges[0], p, result)
+            put_edges(*edges, p, result)
 
 
 def plane_call(kernel, x, sides=(), extras=(), fill=True, edges=False):
@@ -94,15 +96,16 @@
         masks, scale = extras
         specs += [pl.BlockSpec(masks.shape, lambda i: (0, 0, 0)), block(1, cols)]
         args += [masks, scale]
-    out_specs = [block(rows, cols)] * fill + [block(2, rows)] * edges
+    out_specs = [block(rows, cols)] * fill + [block(2, rows), block(2, cols)] * edges
     out_shape = [jax.ShapeDtypeStruct(x.shape, x.dtype)] * fill
-    out_shape += [jax.ShapeDtypeStruct((planes, 2, rows), x.dtype)] * edges
+    out_shape += [jax.ShapeDtypeStruct((planes, 2, side), x.dtype) for side in (rows, cols)] * edges
     return pl.pallas_call(
         kernel,
         grid=(planes // step,),
         in_specs=specs,
         out_specs=out_specs,
         out_shape=out_shape,
+        cost_estimate=pl.CostEstimate(flops=30 * x.size, bytes_accessed=8 * x.size, transcendentals=0),
         compiler_params=pltpu.CompilerParams(vmem_limit_bytes=32 * 1024 * 1024),
     )(*args)
 
@@ -188,18 +191,24 @@
 
 def stiffness_sum(stepped):
     x = stepped.reshape((-1,) + stepped.shape[2:])
-    west, east = row_halo(x)
-    (edges,) = plane_call(edges_kernel, x, fill=False, edges=True)
+    edges, lines = plane_call(edges_kernel, x, fill=False, edges=True)
+    west, east = row_halo(lines[:, 0], lines[:, 1])
     first = column_average(edges[:, 0], west[:, 0], east[:, 0])
     last = column_average(edges[:, 1], west[:, -1], east[:, -1])
     south, north = col_halo(first, last)
-    (out,) = plane_call(stiffness_kernel, x, (west, east, south, north))
-    return out.reshape(stepped.shape)
-
-
-def ocean_halo(x, first, last, gy_index, gy_count):
+    halo = (west, east, south, north)
+    levels = stepped.shape[1]
+    (surface,) = plane_call(
+        stiffness_kernel, x[levels - 1 :: levels], [side[levels - 1 :: levels] for side in halo]
+    )
+    (out,) = plane_call(stiffness_kernel, x, halo)
+    return out.reshape(stepped.shape), surface
+
+
+def ocean_halo(edges, lines, gy_index, gy_count):
     count = lax.axis_size("gx")
-    west, east = row_halo(x)
+    first, last = edges[:, 0], edges[:, 1]
+    west, east = row_halo(lines[:, 0], lines[:, 1])
     south, north = col_halo(first, last)
     mirrored = lax.ppermute(last, "gx", [(i, count - 1 - i) for i in range(count)])
     north = jnp.where(gy_index == gy_count - 1, jnp.flip(mirrored, axis=1), north)
@@ -207,7 +216,9 @@
 
 
 def mask_set(wet, gy_index, gy_count):
-    west, east, south, north = (side[0] for side in ocean_halo(wet[None], wet[None, :, 0], wet[None, :, -1], gy_index, gy_count))
+    edges = jnp.stack([wet[:, 0], wet[:, -1]])[None]
+    lines = jnp.stack([wet[0], wet[-1]])[None]
+    west, east, south, north = (side[0] for side in ocean_halo(edges, lines, gy_index, gy_count))
     south = jnp.where(gy_index == 0, jnp.zeros_like(south), south)
     return jnp.stack(
         [
@@ -223,14 +234,18 @@
 def tracer_steps(tracers, masks, kappa, gy_index, gy_count):
     x = tracers.reshape((-1,) + tracers.shape[2:])
     scale = jnp.broadcast_to(kappa.reshape(-1, 1, 1), (x.shape[0], 1, x.shape[2]))
-    (edges,) = plane_call(edges_kernel, x, fill=False, edges=True)
+    edges, lines = plane_call(edges_kernel, x, fill=False, edges=True)
     for repeat in range(OSUB):
-        halo = ocean_halo(x, edges[:, 0], edges[:, 1], gy_index, gy_count)
+        halo = ocean_halo(edges, lines, gy_index, gy_count)
         if repeat < OSUB - 1:
-            x, edges = plane_call(tracer_kernel, x, halo, (masks, scale), edges=True)
+            x, edges, lines = plane_call(tracer_kernel, x, halo, (masks, scale), edges=True)
         else:
+            levels = tracers.shape[1]
+            (top,) = plane_call(
+                tracer_kernel, x[::levels], [side[::levels] for side in halo], (masks, scale[::levels])
+            )
             (x,) = plane_call(tracer_kernel, x, halo, (masks, scale))
-    return x.reshape(tracers.shape)
+    return x.reshape(tracers.shape), top
 
 
 def per_device(
@@ -250,8 +265,8 @@
     capacity = max(2, 5 * entries // (2 * tile_count))
     slot_total = tile_count * capacity
     stepped = element_step(atm_state, elem_op, column_mix)
-    atm_next = stiffness_sum(stepped)
-    surface = atm_next[:, levels - 1].astype(jnp.bfloat16)
+    atm_next, surface = stiffness_sum(stepped)
+    surface = surface.astype(jnp.bfloat16)
     weights = remap_weight[:, 0]
     products = lax.dot_general(
         weights, surface, (((3,), (2,)), ((0,), (1,))), preferred_element_type=jnp.float32
@@ -297,10 +312,10 @@
     )
     wet_mask = land_mask.astype(jnp.float32)
     masks = mask_set(wet_mask, gy_index, gy_count)
-    tracers = tracer_steps(ocean_state, masks, kappa, gy_index, gy_count)
-    surface_level = tracers[:, 0] + wet_mask * (FLUX_GAIN * forcing)
+    tracers, top = tracer_steps(ocean_state, masks, kappa, gy_index, gy_count)
+    surface_level = top + wet_mask * (FLUX_GAIN * forcing)
     ocean_next = tracers.at[:, 0].set(surface_level)
-    sea_surface = ocean_next[:, 0].astype(jnp.bfloat16)
+    sea_surface = surface_level.astype(jnp.bfloat16)
     back_out = jnp.einsum(
         "lc,flq->cfq",
         receive_map.astype(jnp.bfloat16),

time: 153 us -> 139 us (0.908)
  waiting for transfers between devices: 22.4 us -> 11.4 us
  local copies, waits for them, and re-layouts: 26.5 us -> 20.1 us
  starting transfers between devices: 41.5 us -> 43.9 us
    all_to_all x1, waiting for transfers between devices: 11.4 us -> 1.61 us  [per_device(): lax.all_to_all(back_out.reshape(tile_count, capacity, 2, ocean_cols), ('g...]
    ppermute x8, starting transfers between devices: 16.2 us -> 19.1 us  [the longest x4 18.5 us: row_halo(): lax.ppermute(first, 'gx', [((i + 1) % count, i) for i in range(count)])]
    pallas_call x1 -> x0, local copies, waits for them, and re-layouts: 2.73 us -> none  [element_step(): pl.pallas_call(element_kernel, grid=(variables, row_count // rows), in_sp...]
    pallas_call x2 -> x6, local copies, waits for them, and re-layouts: 2.31 us -> 0.08 us  [plane_call(): pl.pallas_call(kernel, grid=(planes // step,), in_specs=specs, out_specs=...]
    ppermute x4, waiting for transfers between devices: 0.01 us -> 1.92 us  [col_halo(): lax.ppermute(last, 'gy', [(i, (i + 1) % count) for i in range(count)])]
    ppermute x8, waiting for transfers between devices: 9.62 us -> 7.88 us  [the longest x4 5.18 us: row_halo(): lax.ppermute(last, 'gx', [(i, (i + 1) % count) for i in range(count)])]
    pallas_call x5 -> x7, Pallas kernels: 30 us -> 30.5 us  [plane_call(): pl.pallas_call(kernel, grid=(planes // step,), in_specs=specs, out_specs=...]
  transfers between devices with their start and end apart: 21 -> 21, of which waited for: 5 -> 6; matrix products, arithmetic and copies ran while one was open for 14% -> 10% of each run, Pallas kernels for 27% -> 33%
where the time goes in v1:
time: 139 us; the launch traced here: 138 us
  Pallas kernels  44.9 us (32%)
  starting transfers between devices  43.9 us (32%)
  local copies, waits for them, and re-layouts  20.1 us (14%)
  matrix products  14 us (10%)
  waiting for transfers between devices  11.4 us (8%)
  other arithmetic  2.51 us (2%)
    pallas_call x7, Pallas kernels, plane_call(): pl.pallas_call(kernel, grid=(planes // step,), in_specs=specs, out_specs=...  30.5 us
    ppermute x4, starting transfers between devices, row_halo(): lax.ppermute(first, 'gx', [((i + 1) % count, i) for i in range(count)])  18.5 us
    pallas_call x1, Pallas kernels, element_step(): pl.pallas_call(element_kernel, grid=(variables, row_count // rows), in_sp...  14.4 us
    unnamed x26, local copies, waits for them, and re-layouts  13.7 us
    ppermute x3, starting transfers between devices, ocean_halo(): lax.ppermute(last, 'gx', [(i, count - 1 - i) for i in range(count)])  10.8 us
    all_to_all x1, starting transfers between devices, per_device(): lax.all_to_all(back_out.reshape(tile_count, capacity, 2, ocean_cols), ('g...  5.92 us
    dot_general x1, matrix products, per_device(): lax.dot_general(weights, surface, (((3,), (2,)), ((0,), (1,))), preferred...  5.64 us
    ppermute x4, waiting for transfers between devices, row_halo(): lax.ppermute(last, 'gx', [(i, (i + 1) % count) for i in range(count)])  5.18 us
  transfers between devices with their start and end apart: 21, of which 6 were waited for; matrix products, arithmetic and copies ran while one was open for 10% of the time, Pallas kernels for 33%

profile of v1, /device:TPU:0, one launch (start us, length us, event | category | flops | bytes accessed | tf_op | source)
XLA Modules:
  0.0 138.1 jit_solution(7245026234435994822)
XLA Ops:
  0.7 0.8 convert_element_type.48
  1.4 0.2 slice_reduce_fusion.2
  1.6 6.1 %collective-permute-start.11 = (f32[1,64]{1,0:T(1,128)S(1)}, f32[1,64]{1,0:T(1,128)S(1)}, u32[]{:S(2)}, u32[]{:S(2)}) collective-permute-start(f32[1,64]{1,0:T(1,128)S(1)} %get-tuple-element.75), channel_id=1, source_target_pairs={{0,28},{4,24},{8,20},{12,16},{16,12},{20,8},{24,4},{28,0},{1,29},{... | collective-permute-start | bytes 776 | tf_op jit(solution)/shard_map/ppermute | solution.py:213
  7.7 2.1 %copy-done.2 = f32[2,60,64,128]{3,2,1,0:T(8,128)S(1)} copy-done((f32[2,60,64,128]{3,2,1,0:T(8,128)S(1)}, f32[2,60,64,128]{3,2,1,0:T(8,128)}, u32[]{:S(2)}) %copy-start.2) | copy-done | bytes 3932184
  9.8 2.7 %shard_map.106 = (f32[120,2,64]{2,1,0:T(2,128)S(1)}, f32[120,2,128]{2,1,0:T(2,128)S(1)}) custom-call(f32[120,64,128]{2,1,0:T(8,128)S(1)} %bitcast.178), custom_call_target="tpu_custom_call" | custom-call | flops 29491200 | bytes 7864320 | tf_op jit(solution)/shard_map/pallas_call | solution.py:102
  12.6 0.1 collective-permute-start.7
  12.8 1.6 %collective-permute-start.6 = (f32[120,64]{1,0:T(8,128)S(1)}, f32[120,64]{1,0:T(8,128)S(1)}, u32[]{:S(2)}, u32[]{:S(2)}) collective-permute-start(f32[120,64]{1,0:T(8,128)S(1)} %get-tuple-element.60), channel_id=1, source_target_pairs={{0,1},{1,2},{2,3},{3,0},{4,5},{5,6},{6,7},{7,4},{8,9},{9,10},{10,1... | collective-permute-start | bytes 92168 | tf_op jit(solution)/shard_map/ppermute | solution.py:25
  14.3 0.2 collective-permute-start.12
  14.7 2.3 %copy-done.4 = f32[2,72,64,128]{3,2,1,0:T(8,128)S(1)} copy-done((f32[2,72,64,128]{3,2,1,0:T(8,128)S(1)}, f32[2,72,64,128]{3,2,1,0:T(8,128)}, u32[]{:S(2)}) %copy-start.4) | copy-done | bytes 4718616
  17.1 14.4 %shard_map.103 = f32[2,72,64,128]{3,2,1,0:T(8,128)S(1)} custom-call(f32[2,72,64,128]{3,2,1,0:T(8,128)S(1)} %copy-done.4, f32[16,16]{1,0:T(8,128)S(1)} %bitcast.186, f32[72,72]{1,0:T(8,128)S(1)} %copy-done.7), custom_call_target="tpu_custom_call" | custom-call | tf_op jit(solution)/shard_map/pallas_call | solution.py:166
  31.5 3.3 %shard_map.104 = (f32[144,2,64]{2,1,0:T(2,128)S(1)}, f32[144,2,128]{2,1,0:T(2,128)S(1)}) custom-call(f32[144,64,128]{2,1,0:T(8,128)S(1)} %bitcast.175), custom_call_target="tpu_custom_call" | custom-call | flops 35389440 | bytes 9437184 | tf_op jit(solution)/shard_map/pallas_call | solution.py:102
  34.9 0.1 reshape.305
  35.0 0.4 copy.232
  35.4 0.7 reshape.306
  36.1 0.7 broadcast_in_dim_reshape.3
  37.0 0.1 copy.226
  37.1 0.1 reshape.303
  37.2 0.2 convert_reduce_fusion
  37.5 0.6 reduce-window.6
  38.1 0.2 slice_reduce_fusion
  38.3 0.1 bitcast_subtract_fusion
  38.4 1.2 bitcast_convert_fusion
  39.7 0.1 slice.202
  39.9 4.6 %collective-permute-start.9 = (f32[1,128]{1,0:T(1,128)S(1)}, f32[1,128]{1,0:T(1,128)S(1)}, u32[]{:S(2)}, u32[]{:S(2)}) collective-permute-start(f32[1,128]{1,0:T(1,128)S(1)} %get-tuple-element.77), channel_id=1, source_target_pairs={{4,0},{8,4},{12,8},{16,12},{20,16},{24,20},{28,24},{0,28},{5,1},{9... | collective-permute-start | bytes 1544 | tf_op jit(solution)/shard_map/ppermute | solution.py:19
  44.5 0.1 rev.12
  44.7 0.1 copy.214
  44.8 0.1 copy.215
  44.9 0.9 collective-permute-done.9
  45.8 4.9 %collective-permute-start.1 = (f32[144,128]{1,0:T(8,128)S(1)}, f32[144,128]{1,0:T(8,128)S(1)}, u32[]{:S(2)}, u32[]{:S(2)}) collective-permute-start(f32[144,128]{1,0:T(8,128)S(1)} %get-tuple-element.53), channel_id=1, source_target_pairs={{4,0},{8,4},{12,8},{16,12},{20,16},{24,20},{28,24},{0,28},{5,1},{9... | collective-permute-start | bytes 221192 | tf_op jit(solution)/shard_map/ppermute | solution.py:19
  50.7 0.1 collective-permute-done.10
  50.9 1.8 %collective-permute-done.1 = f32[144,128]{1,0:T(8,128)S(1)} collective-permute-done((f32[144,128]{1,0:T(8,128)S(1)}, f32[144,128]{1,0:T(8,128)S(1)}, u32[]{:S(2)}, u32[]{:S(2)}) %collective-permute-start.1) | collective-permute-done | bytes 73760 | tf_op jit(solution)/shard_map/ppermute | solution.py:19
  52.8 5.1 %collective-permute-done = f32[144,128]{1,0:T(8,128)S(1)} collective-permute-done((f32[144,128]{1,0:T(8,128)S(1)}, f32[144,128]{1,0:T(8,128)S(1)}, u32[]{:S(2)}, u32[]{:S(2)}) %collective-permute-start) | collective-permute-done | bytes 73760 | tf_op jit(solution)/shard_map/ppermute | solution.py:18
  58.0 0.2 fusion.40
  58.2 1.7 %collective-permute-start.3 = (f32[144,64]{1,0:T(8,128)S(1)}, f32[144,64]{1,0:T(8,128)S(1)}, u32[]{:S(2)}, u32[]{:S(2)}) collective-permute-start(f32[144,64]{1,0:T(8,128)S(1)} %get-tuple-element.79), channel_id=1, source_target_pairs={{1,0},{2,1},{3,2},{0,3},{5,4},{6,5},{7,6},{4,7},{9,8},{10,9},{11,1... | collective-permute-start | bytes 110600 | tf_op jit(solution)/shard_map/ppermute | solution.py:26
  60.1 1.9 %collective-permute-done.2 = f32[144,64]{1,0:T(8,128)S(1)} collective-permute-done((f32[144,64]{1,0:T(8,128)S(1)}, f32[144,64]{1,0:T(8,128)S(1)}, u32[]{:S(2)}, u32[]{:S(2)}) %collective-permute-start.2) | collective-permute-done | bytes 36896 | tf_op jit(solution)/shard_map/ppermute | solution.py:25
  62.0 4.8 %collective-permute-start.5 = (f32[120,128]{1,0:T(8,128)S(1)}, f32[120,128]{1,0:T(8,128)S(1)}, u32[]{:S(2)}, u32[]{:S(2)}) collective-permute-start(f32[120,128]{1,0:T(8,128)S(1)} %get-tuple-element.61), channel_id=1, source_target_pairs={{4,0},{8,4},{12,8},{16,12},{20,16},{24,20},{28,24},{0,28},{5,1},{9... | collective-permute-start | bytes 184328 | tf_op jit(solution)/shard_map/ppermute | solution.py:19
  66.8 0.3 shard_map.110
  67.1 5.6 %fusion.2 = f32[64,2,4,128]{3,1,2,0:T(2,128)S(1)} fusion(bf16[64,1,4,128,128]{4,3,2,1,0:T(8,128)(2,1)} %param.16, bf16[2,64,128,1]{2,1,0,3:T(8,128)(2,1)S(1)} %convert_bitcast_fusion), kind=kOutput, calls=%fused_computation.2 | convolution fusion | flops 16777216 | bytes 8683520 | tf_op jit(solution)/shard_map/dot_general | solution.py:271
  72.7 0.5 fusion.13
  73.2 1.4 copy.231
  74.6 2.6 %all-to-all-start = ((f32[32,20,2,128]{3,2,1,0:T(2,128)}), f32[32,20,2,128]{3,2,1,0:T(2,128)S(1)}, u32[]{:S(2)}, u32[]{:S(2)}) async-start(f32[32,20,2,128]{3,2,1,0:T(2,128)} %copy.231), calls=%async_computation | async-start | bytes 1310720 | tf_op jit(solution)/shard_map/all_to_all | solution.py:300
  77.5 0.2 broadcast_in_dim.95.kappa_ref
  77.7 2.1 %copy-done.3 = f32[2,60,64,128]{3,2,1,0:T(8,128)S(1)} copy-done((f32[2,60,64,128]{3,2,1,0:T(8,128)S(1)}, f32[2,60,64,128]{3,2,1,0:T(8,128)}, u32[]{:S(2)}) %copy-start.3) | copy-done | bytes 3932184
  79.8 9.3 %shard_map.107 = (f32[120,64,128]{2,1,0:T(8,128)S(1)}, f32[120,2,64]{2,1,0:T(2,128)S(1)}, f32[120,2,128]{2,1,0:T(2,128)S(1)}) custom-call(f32[120,64,128]{2,1,0:T(8,128)S(1)} %bitcast.179, f32[120,1,128]{2,1,0:T(1,128)S(1)} %bitcast.184, f32[120,1,128]{2,1,0:T(1,128)S(1)} %bitcast.185, f32[120,2,64]{2,1,0:T(2,128)S(1)} %copy.216.cols_ref, ...), custom_call_target="tpu_custom_call" | custom-call | flops 29491200 | bytes 7864320 | tf_op jit(solution)/shard_map/pallas_call | solution.py:102
  89.2 4.6 %collective-permute-start.17 = (f32[120,64]{1,0:T(8,128)S(1)}, f32[120,64]{1,0:T(8,128)S(1)}, u32[]{:S(2)}, u32[]{:S(2)}) collective-permute-start(f32[120,64]{1,0:T(8,128)S(1)} %get-tuple-element.56), channel_id=1, source_target_pairs={{0,28},{4,24},{8,20},{12,16},{16,12},{20,8},{24,4},{28,0},{1,29},{... | collective-permute-start | bytes 92168 | tf_op jit(solution)/shard_map/ppermute | solution.py:213
  93.8 1.7 %collective-permute-start.18 = (f32[120,64]{1,0:T(8,128)S(1)}, f32[120,64]{1,0:T(8,128)S(1)}, u32[]{:S(2)}, u32[]{:S(2)}) collective-permute-start(f32[120,64]{1,0:T(8,128)S(1)} %get-tuple-element.55), channel_id=1, source_target_pairs={{1,0},{2,1},{3,2},{0,3},{5,4},{6,5},{7,6},{4,7},{9,8},{10,9},{11,1... | collective-permute-start | bytes 92168 | tf_op jit(solution)/shard_map/ppermute | solution.py:26
  95.6 0.6 collective-permute-start.14
  96.2 4.2 %collective-permute-start.15 = (f32[120,128]{1,0:T(8,128)S(1)}, f32[120,128]{1,0:T(8,128)S(1)}, u32[]{:S(2)}, u32[]{:S(2)}) collective-permute-start(f32[120,128]{1,0:T(8,128)S(1)} %get-tuple-element.57), channel_id=1, source_target_pairs={{4,0},{8,4},{12,8},{16,12},{20,16},{24,20},{28,24},{0,28},{5,1},{9... | collective-permute-start | bytes 184328 | tf_op jit(solution)/shard_map/ppermute | solution.py:19
  100.4 1.9 %copy-done.5 = f32[120,64,128]{2,1,0:T(8,128)} copy-done((f32[120,64,128]{2,1,0:T(8,128)}, f32[120,64,128]{2,1,0:T(8,128)S(1)}, u32[]{:S(2)}) %copy-start.5) | copy-done | bytes 3932184
  102.4 0.1 pad_maximum_fusion.2.cols_ref
  102.7 0.2 shard_map.109
  103.0 2.1 %copy-done.6 = f32[120,64,128]{2,1,0:T(8,128)S(1)} copy-done((f32[120,64,128]{2,1,0:T(8,128)S(1)}, f32[120,64,128]{2,1,0:T(8,128)}, u32[]{:S(2)}) %copy-start.6) | copy-done | bytes 3932184
  105.1 6.7 %shard_map.108 = f32[120,64,128]{2,1,0:T(8,128)} custom-call(f32[120,64,128]{2,1,0:T(8,128)S(1)} %copy-done.6, f32[120,1,128]{2,1,0:T(1,128)S(1)} %bitcast.182, f32[120,1,128]{2,1,0:T(1,128)S(1)} %bitcast.183, f32[120,2,64]{2,1,0:T(2,128)S(1)} %pad_maximum_fusion.2.cols_ref, f32[5,64,128]{2,1,0:T(8,128)S(1)} %bitcast_dynamic-update-slice_fusion.1.masks_ref, ...), custom_call_target="tpu_custom_call" | custom-call | flops 29491200 | bytes 7864320 | tf_op jit(solution)/shard_map/pallas_call | solution.py:102
  111.8 1.5 %bitcast_dynamic-update-slice_fusion = (f32[2,60,64,128]{3,2,1,0:T(8,128)}, f32[2,64,128]{2,1,0:T(8,128)S(1)}) fusion(f32[2,60,64,128]{3,2,1,0:T(8,128)} %bitcast.194, f32[2,64,128]{2,1,0:T(8,128)S(1)} %shard_map.109, f32[64,128]{1,0:T(8,128)S(1)} %broadcast_multiply_fusion, f32[32,64,20]{1,2,0:T(8,128)S(1)} %get-tuple-element.83, ...), kind=kOutput, calls=%fused_computation.61 | convolution fusion | flops 125861888 | bytes 1048576 | tf_op jit(solution)/shard_map/lc,cfq->flq/dot_general | solution.py:307
  113.3 0.2 convolution_convert_fusion
  113.5 1.1 copy.241
  114.6 5.9 %all-to-all-start.1 = ((bf16[32,20,2,128]{3,2,1,0:T(2,128)(2,1)}), bf16[32,20,2,128]{3,2,1,0:T(2,128)(2,1)S(1)}, u32[]{:S(2)}, u32[]{:S(2)}) async-start(bf16[32,20,2,128]{3,2,1,0:T(2,128)(2,1)} %bitcast.77), calls=%async_computation.1 | async-start | bytes 655360 | tf_op jit(solution)/shard_map/all_to_all | solution.py:325
  120.5 0.2 pad_maximum_fusion.cols_ref
  120.7 2.3 %copy-done.1 = f32[2,72,64,128]{3,2,1,0:T(8,128)S(1)} copy-done((f32[2,72,64,128]{3,2,1,0:T(8,128)S(1)}, f32[2,72,64,128]{3,2,1,0:T(8,128)}, u32[]{:S(2)}) %copy-start.1) | copy-done | bytes 4718616
  123.0 7.9 %shard_map.105 = f32[144,64,128]{2,1,0:T(8,128)} custom-call(f32[144,64,128]{2,1,0:T(8,128)S(1)} %bitcast.177, f32[144,1,128]{2,1,0:T(1,128)S(1)} %bitcast.181, f32[144,1,128]{2,1,0:T(1,128)S(1)} %bitcast.180, f32[144,2,64]{2,1,0:T(2,128)S(1)} %pad_maximum_fusion.cols_ref), custom_call_target="tpu_custom_call" | custom-call | flops 35389440 | bytes 9437184 | tf_op jit(solution)/shard_map/pallas_call | solution.py:102
  130.9 1.6 %all-to-all-done.1 = bf16[32,20,2,128]{3,2,1,0:T(2,128)(2,1)S(1)} async-done(((bf16[32,20,2,128]{3,2,1,0:T(2,128)(2,1)}), bf16[32,20,2,128]{3,2,1,0:T(2,128)(2,1)S(1)}, u32[]{:S(2)}, u32[]{:S(2)}) %all-to-all-start.1) | async-done | bytes 327712 | tf_op jit(solution)/shard_map/all_to_all | solution.py:325
  132.5 0.3 convolution_convert_fusion.1
  132.8 4.7 %fusion.5 = f32[2,64,128]{2,0,1:T(2,128)S(1)} fusion(bf16[64,1,4,128,128]{4,3,2,1,0:T(8,128)(2,1)} %param.16, bf16[64,4,2,128]{3,1,0,2:T(4,128)(2,1)S(1)} %bitcast.196), kind=kOutput, calls=%fused_computation.8 | convolution fusion | flops 16777216 | bytes 8585216 | tf_op jit(solution)/shard_map/dot_general | solution.py:339
  137.5 0.6 copy.244
  (100 shorter events, 1.7 us)
Async XLA Ops:
  0.6 14.0 %copy-start.10 = (f32[16,16]{1,0:T(8,128)S(1)}, f32[16,16]{1,0:T(8,128)}, u32[]{:S(2)}) copy-start(f32[16,16]{1,0:T(8,128)} %param.13) | copy-start | bytes 3076
  0.6 14.1 %copy-start.7 = (f32[72,72]{1,0:T(8,128)S(1)}, f32[72,72]{1,0:T(8,128)}, u32[]{:S(2)}) copy-start(f32[72,72]{1,0:T(8,128)} %mix_ref.1) | copy-start | bytes 62212
  1.6 38.2 %collective-permute-start.11 = (f32[1,64]{1,0:T(1,128)S(1)}, f32[1,64]{1,0:T(1,128)S(1)}, u32[]{:S(2)}, u32[]{:S(2)}) collective-permute-start(f32[1,64]{1,0:T(1,128)S(1)} %get-tuple-element.75), channel_id=1, source_target_pairs={{0,28},{4,24},{8,20},{12,16},{16,12},{20,8},{24,4},{28,0},{1,29},{... | collective-permute-start | bytes 776 | tf_op jit(solution)/shard_map/ppermute | solution.py:213
  7.7 36.9 %collective-permute-start.13 = (f32[1,64]{1,0:T(1,128)S(1)}, f32[1,64]{1,0:T(1,128)S(1)}, u32[]{:S(2)}, u32[]{:S(2)}) collective-permute-start(f32[1,64]{1,0:T(1,128)S(1)} %get-tuple-element.75), channel_id=1, source_target_pairs={{0,1},{1,2},{2,3},{3,0},{4,5},{5,6},{6,7},{7,4},{8,9},{9,10},{10,1... | collective-permute-start | bytes 776 | tf_op jit(solution)/shard_map/ppermute | solution.py:25
  7.7 2.1 %copy-start.2 = (f32[2,60,64,128]{3,2,1,0:T(8,128)S(1)}, f32[2,60,64,128]{3,2,1,0:T(8,128)}, u32[]{:S(2)}) copy-start(f32[2,60,64,128]{3,2,1,0:T(8,128)} %param.11) | copy-start | bytes 11796484
  12.6 64.6 %collective-permute-start.7 = (f32[120,64]{1,0:T(8,128)S(1)}, f32[120,64]{1,0:T(8,128)S(1)}, u32[]{:S(2)}, u32[]{:S(2)}) collective-permute-start(f32[120,64]{1,0:T(8,128)S(1)} %get-tuple-element.60), channel_id=1, source_target_pairs={{0,28},{4,24},{8,20},{12,16},{16,12},{20,8},{24,4},{28,0},{1,29},{... | collective-permute-start | bytes 92168 | tf_op jit(solution)/shard_map/ppermute | solution.py:213
  12.8 64.6 %collective-permute-start.6 = (f32[120,64]{1,0:T(8,128)S(1)}, f32[120,64]{1,0:T(8,128)S(1)}, u32[]{:S(2)}, u32[]{:S(2)}) collective-permute-start(f32[120,64]{1,0:T(8,128)S(1)} %get-tuple-element.60), channel_id=1, source_target_pairs={{0,1},{1,2},{2,3},{3,0},{4,5},{5,6},{6,7},{7,4},{8,9},{9,10},{10,1... | collective-permute-start | bytes 92168 | tf_op jit(solution)/shard_map/ppermute | solution.py:25
  14.3 30.3 %collective-permute-start.12 = (f32[1,64]{1,0:T(1,128)S(1)}, f32[1,64]{1,0:T(1,128)S(1)}, u32[]{:S(2)}, u32[]{:S(2)}) collective-permute-start(f32[1,64]{1,0:T(1,128)S(1)} %get-tuple-element.74), channel_id=1, source_target_pairs={{1,0},{2,1},{3,2},{0,3},{5,4},{6,5},{7,6},{4,7},{9,8},{10,9},{11,1... | collective-permute-start | bytes 776 | tf_op jit(solution)/shard_map/ppermute | solution.py:26
  14.7 2.3 %copy-start.4 = (f32[2,72,64,128]{3,2,1,0:T(8,128)S(1)}, f32[2,72,64,128]{3,2,1,0:T(8,128)}, u32[]{:S(2)}) copy-start(f32[2,72,64,128]{3,2,1,0:T(8,128)} %x_ref.1) | copy-start | bytes 14155780
  31.5 3.4 %copy-start = (f32[2,72,64,128]{3,2,1,0:T(8,128)}, f32[2,72,64,128]{3,2,1,0:T(8,128)S(1)}, u32[]{:S(2)}) copy-start(f32[2,72,64,128]{3,2,1,0:T(8,128)S(1)} %shard_map.103) | copy-start | bytes 14155780
  31.5 3.4 %copy-start.9 = (s32[512,4,4]{0,2,1:T(4,128)S(1)}, s32[512,4,4]{0,2,1:T(4,128)}, u32[]{:S(2)}) copy-start(s32[512,4,4]{0,2,1:T(4,128)} %param.17) | copy-start | bytes 98308
  31.5 5.2 %copy-start.8 = (s32[64,128]{1,0:T(8,128)S(1)}, s32[64,128]{1,0:T(8,128)}, u32[]{:S(2)}) copy-start(s32[64,128]{1,0:T(8,128)} %param.12) | copy-start | bytes 98308
  34.9 4.7 %copy-start.11 = (f32[2,60]{1,0:T(2,128)S(1)}, f32[2,60]{1,0:T(2,128)}, u32[]{:S(2)}) copy-start(f32[2,60]{1,0:T(2,128)} %param.15) | copy-start | bytes 1444
  39.9 5.9 %collective-permute-start.9 = (f32[1,128]{1,0:T(1,128)S(1)}, f32[1,128]{1,0:T(1,128)S(1)}, u32[]{:S(2)}, u32[]{:S(2)}) collective-permute-start(f32[1,128]{1,0:T(1,128)S(1)} %get-tuple-element.77), channel_id=1, source_target_pairs={{4,0},{8,4},{12,8},{16,12},{20,16},{24,20},{28,24},{0,28},{5,1},{9... | collective-permute-start | bytes 1544 | tf_op jit(solution)/shard_map/ppermute | solution.py:19
  44.6 6.2 %collective-permute-start.10 = (f32[1,128]{1,0:T(1,128)S(1)}, f32[1,128]{1,0:T(1,128)S(1)}, u32[]{:S(2)}, u32[]{:S(2)}) collective-permute-start(f32[1,128]{1,0:T(1,128)S(1)} %get-tuple-element.76), channel_id=1, source_target_pairs={{0,4},{4,8},{8,12},{12,16},{16,20},{20,24},{24,28},{28,0},{1,5},{5... | collective-permute-start | bytes 1544 | tf_op jit(solution)/shard_map/ppermute | solution.py:18
  44.6 32.7 %collective-permute-start.8 = (f32[120,64]{1,0:T(8,128)S(1)}, f32[120,64]{1,0:T(8,128)S(1)}, u32[]{:S(2)}, u32[]{:S(2)}) collective-permute-start(f32[120,64]{1,0:T(8,128)S(1)} %get-tuple-element.59), channel_id=1, source_target_pairs={{1,0},{2,1},{3,2},{0,3},{5,4},{6,5},{7,6},{4,7},{9,8},{10,9},{11,1... | collective-permute-start | bytes 92168 | tf_op jit(solution)/shard_map/ppermute | solution.py:26
  45.8 6.9 %collective-permute-start.1 = (f32[144,128]{1,0:T(8,128)S(1)}, f32[144,128]{1,0:T(8,128)S(1)}, u32[]{:S(2)}, u32[]{:S(2)}) collective-permute-start(f32[144,128]{1,0:T(8,128)S(1)} %get-tuple-element.53), channel_id=1, source_target_pairs={{4,0},{8,4},{12,8},{16,12},{20,16},{24,20},{28,24},{0,28},{5,1},{9... | collective-permute-start | bytes 221192 | tf_op jit(solution)/shard_map/ppermute | solution.py:19
  50.8 7.0 %collective-permute-start = (f32[144,128]{1,0:T(8,128)S(1)}, f32[144,128]{1,0:T(8,128)S(1)}, u32[]{:S(2)}, u32[]{:S(2)}) collective-permute-start(f32[144,128]{1,0:T(8,128)S(1)} %get-tuple-element.54), channel_id=1, source_target_pairs={{0,4},{4,8},{8,12},{12,16},{16,20},{20,24},{24,28},{28,0},{1,5},{5... | collective-permute-start | bytes 221192 | tf_op jit(solution)/shard_map/ppermute | solution.py:18
  58.2 3.8 %collective-permute-start.2 = (f32[144,64]{1,0:T(8,128)S(1)}, f32[144,64]{1,0:T(8,128)S(1)}, u32[]{:S(2)}, u32[]{:S(2)}) collective-permute-start(f32[144,64]{1,0:T(8,128)S(1)} %get-tuple-element.78), channel_id=1, source_target_pairs={{0,1},{1,2},{2,3},{3,0},{4,5},{5,6},{6,7},{7,4},{8,9},{9,10},{10,1... | collective-permute-start | bytes 110600 | tf_op jit(solution)/shard_map/ppermute | solution.py:25
  58.2 3.8 %collective-permute-start.3 = (f32[144,64]{1,0:T(8,128)S(1)}, f32[144,64]{1,0:T(8,128)S(1)}, u32[]{:S(2)}, u32[]{:S(2)}) collective-permute-start(f32[144,64]{1,0:T(8,128)S(1)} %get-tuple-element.79), channel_id=1, source_target_pairs={{1,0},{2,1},{3,2},{0,3},{5,4},{6,5},{7,6},{4,7},{9,8},{10,9},{11,1... | collective-permute-start | bytes 110600 | tf_op jit(solution)/shard_map/ppermute | solution.py:26
  62.0 15.5 %collective-permute-start.4 = (f32[120,128]{1,0:T(8,128)S(1)}, f32[120,128]{1,0:T(8,128)S(1)}, u32[]{:S(2)}, u32[]{:S(2)}) collective-permute-start(f32[120,128]{1,0:T(8,128)S(1)} %get-tuple-element.62), channel_id=1, source_target_pairs={{0,4},{4,8},{8,12},{12,16},{16,20},{20,24},{24,28},{28,0},{1,5},{5... | collective-permute-start | bytes 184328 | tf_op jit(solution)/shard_map/ppermute | solution.py:18
  62.0 15.4 %collective-permute-start.5 = (f32[120,128]{1,0:T(8,128)S(1)}, f32[120,128]{1,0:T(8,128)S(1)}, u32[]{:S(2)}, u32[]{:S(2)}) collective-permute-start(f32[120,128]{1,0:T(8,128)S(1)} %get-tuple-element.61), channel_id=1, source_target_pairs={{4,0},{8,4},{12,8},{16,12},{20,16},{24,20},{28,24},{0,28},{5,1},{9... | collective-permute-start | bytes 184328 | tf_op jit(solution)/shard_map/ppermute | solution.py:19
  74.6 37.2 %all-to-all-start = ((f32[32,20,2,128]{3,2,1,0:T(2,128)}), f32[32,20,2,128]{3,2,1,0:T(2,128)S(1)}, u32[]{:S(2)}, u32[]{:S(2)}) async-start(f32[32,20,2,128]{3,2,1,0:T(2,128)} %copy.231), calls=%async_computation | async-start | bytes 1310720 | tf_op jit(solution)/shard_map/all_to_all | solution.py:300
  77.7 2.1 %copy-start.3 = (f32[2,60,64,128]{3,2,1,0:T(8,128)S(1)}, f32[2,60,64,128]{3,2,1,0:T(8,128)}, u32[]{:S(2)}) copy-start(f32[2,60,64,128]{3,2,1,0:T(8,128)} %param.11) | copy-start | bytes 11796484
  89.2 13.1 %collective-permute-start.17 = (f32[120,64]{1,0:T(8,128)S(1)}, f32[120,64]{1,0:T(8,128)S(1)}, u32[]{:S(2)}, u32[]{:S(2)}) collective-permute-start(f32[120,64]{1,0:T(8,128)S(1)} %get-tuple-element.56), channel_id=1, source_target_pairs={{0,28},{4,24},{8,20},{12,16},{16,12},{20,8},{24,4},{28,0},{1,29},{... | collective-permute-start | bytes 92168 | tf_op jit(solution)/shard_map/ppermute | solution.py:213
  93.8 8.6 %collective-permute-start.16 = (f32[120,64]{1,0:T(8,128)S(1)}, f32[120,64]{1,0:T(8,128)S(1)}, u32[]{:S(2)}, u32[]{:S(2)}) collective-permute-start(f32[120,64]{1,0:T(8,128)S(1)} %get-tuple-element.56), channel_id=1, source_target_pairs={{0,1},{1,2},{2,3},{3,0},{4,5},{5,6},{6,7},{7,4},{8,9},{9,10},{10,1... | collective-permute-start | bytes 92168 | tf_op jit(solution)/shard_map/ppermute | solution.py:25
  93.8 8.6 %collective-permute-start.18 = (f32[120,64]{1,0:T(8,128)S(1)}, f32[120,64]{1,0:T(8,128)S(1)}, u32[]{:S(2)}, u32[]{:S(2)}) collective-permute-start(f32[120,64]{1,0:T(8,128)S(1)} %get-tuple-element.55), channel_id=1, source_target_pairs={{1,0},{2,1},{3,2},{0,3},{5,4},{6,5},{7,6},{4,7},{9,8},{10,9},{11,1... | collective-permute-start | bytes 92168 | tf_op jit(solution)/shard_map/ppermute | solution.py:26
  95.6 7.0 %collective-permute-start.14 = (f32[120,128]{1,0:T(8,128)S(1)}, f32[120,128]{1,0:T(8,128)S(1)}, u32[]{:S(2)}, u32[]{:S(2)}) collective-permute-start(f32[120,128]{1,0:T(8,128)S(1)} %get-tuple-element.58), channel_id=1, source_target_pairs={{0,4},{4,8},{8,12},{12,16},{16,20},{20,24},{24,28},{28,0},{1,5},{5... | collective-permute-start | bytes 184328 | tf_op jit(solution)/shard_map/ppermute | solution.py:18
  96.2 6.5 %collective-permute-start.15 = (f32[120,128]{1,0:T(8,128)S(1)}, f32[120,128]{1,0:T(8,128)S(1)}, u32[]{:S(2)}, u32[]{:S(2)}) collective-permute-start(f32[120,128]{1,0:T(8,128)S(1)} %get-tuple-element.57), channel_id=1, source_target_pairs={{4,0},{8,4},{12,8},{16,12},{20,16},{24,20},{28,24},{0,28},{5,1},{9... | collective-permute-start | bytes 184328 | tf_op jit(solution)/shard_map/ppermute | solution.py:19
  100.4 1.9 %copy-start.5 = (f32[120,64,128]{2,1,0:T(8,128)}, f32[120,64,128]{2,1,0:T(8,128)S(1)}, u32[]{:S(2)}) copy-start(f32[120,64,128]{2,1,0:T(8,128)S(1)} %get-tuple-element.26.x_ref) | copy-start | bytes 11796484
  103.0 2.1 %copy-start.6 = (f32[120,64,128]{2,1,0:T(8,128)S(1)}, f32[120,64,128]{2,1,0:T(8,128)}, u32[]{:S(2)}) copy-start(f32[120,64,128]{2,1,0:T(8,128)} %copy-done.5) | copy-start | bytes 11796484
  114.6 17.9 %all-to-all-start.1 = ((bf16[32,20,2,128]{3,2,1,0:T(2,128)(2,1)}), bf16[32,20,2,128]{3,2,1,0:T(2,128)(2,1)S(1)}, u32[]{:S(2)}, u32[]{:S(2)}) async-start(bf16[32,20,2,128]{3,2,1,0:T(2,128)(2,1)} %bitcast.77), calls=%async_computation.1 | async-start | bytes 655360 | tf_op jit(solution)/shard_map/all_to_all | solution.py:325
  120.7 2.3 %copy-start.1 = (f32[2,72,64,128]{3,2,1,0:T(8,128)S(1)}, f32[2,72,64,128]{3,2,1,0:T(8,128)}, u32[]{:S(2)}) copy-start(f32[2,72,64,128]{3,2,1,0:T(8,128)} %copy-done) | copy-start | bytes 14155780
